TPU v7x, 32 devices: a whole 2x2x4 slice. The times are simulated.
32 devices in a mesh: af: 4 (over z), row: 8 (over y, x, core).
Axes of the slice: x: 2, y: 2, z: 4, core: 2. Of those that a mesh axis runs over, the one named last changes fastest.
Arguments:
- image_in: bfloat16 [10, 2, 20, 256, 256], P(None, None, 'af', 'row'), may hold values from -6 to 6
- measured: float32 [10, 20, 256, 512], P(None, None, ('af', 'row')), may hold values from -6 to 6
- target: float32 [10, 20, 256, 512], P(None, None, ('af', 'row')), may hold values from -6 to 6
- line_mask: int32 [20, 256], P(None, ('af', 'row')), may hold values from 0 to 1, as said below
- window_half: int32 [20], replicated, may hold values from 0 to 2
- in_kernel: float32 [64, 54], replicated, may hold values from -0.875 to 0.875
- out_kernel: float32 [27, 2, 64], replicated, may hold values from -0.15625 to 0.15625
- biases: float32 [66], replicated, may hold values from -1 to 1
- in_moment: float32 [64, 54], replicated, may hold values from -0.00012207031 to 0.00012207031
- out_moment: float32 [27, 2, 64], replicated, may hold values from -0.00061035156 to 0.00061035156
- bias_moment: float32 [66], replicated, may hold values from -0.0004272461 to 0.0004272461
- in_square: float32 [64, 54], replicated, may hold values from 6.866455e-11 to 2.746582e-10
- out_square: float32 [27, 2, 64], replicated, may hold values from 1.7166137e-09 to 6.866455e-09
- bias_square: float32 [66], replicated, may hold values from 7.6293943e-10 to 3.0517577e-09
- in_smooth: float32 [64, 54], replicated, may hold values from -0.875 to 0.875
- out_smooth: float32 [27, 2, 64], replicated, may hold values from -0.15625 to 0.15625
- bias_smooth: float32 [66], replicated, may hold values from -1 to 1
Outputs:
- loss_total: float32 [], replicated
- unsampled_count: float32 [], replicated
- in_first: float32 [64, 54], replicated
- out_first: float32 [27, 2, 64], replicated
- bias_first: float32 [66], replicated
- in_second: float32 [64, 54], replicated
- out_second: float32 [27, 2, 64], replicated
- bias_second: float32 [66], replicated
- in_master: float32 [64, 54], replicated
- out_master: float32 [27, 2, 64], replicated
- bias_master: float32 [66], replicated
- in_average: float32 [64, 54], replicated
- out_average: float32 [27, 2, 64], replicated
- bias_average: float32 [66], replicated
- in_copy: bfloat16 [64, 54], replicated
- out_copy: bfloat16 [27, 2, 64], replicated
- bias_copy: bfloat16 [66], replicated
Inputs may be any that keep to these rules, and one draw needn't show every extreme that they name: `line_mask`: 1 where line ky of frame t is sampled; line 256 - 1 is unsampled in every frame.
All inputs are finite; a program needn't handle non-finite values.
Results may differ from a plain program's by a relative error of at most 0.004.
The roundings to bfloat16 on the way count: a program that leaves them out, or rounds other values in their place, can miss the bound.
Values may be sent and summed in bfloat16 or wider, within the bound.
No kernel may reach another device: no remote copies, remote signals or barrier semaphores. Data moves between devices by JAX's collectives and lax.ppermute only.
A program may use at most 128 MiB of HBM per device.

v0:
```python
import math

import jax
import jax.numpy as jnp
from jax import lax
from jax.sharding import PartitionSpec as P

MICRO = 10
STEP = 5


beta_first = 0.5
beta_second = 0.5
rate_in = 0.2
rate_out = 0.04
rate_bias = 0.3
decay_weight = 0.01
average_keep = 0.9
epsilon = 1e-08


def with_halo(block, sides, width):
    for axis, dim in sides:
        count = lax.axis_size(axis)
        forward = [(i, i + 1) for i in range(count - 1)]
        backward = [(target, source) for source, target in forward]
        low = lax.ppermute(
            lax.slice_in_dim(block, block.shape[dim] - width, None, axis=dim), axis, forward
        )
        high = lax.ppermute(lax.slice_in_dim(block, 0, width, axis=dim), axis, backward)
        block = jnp.concatenate([low, block, high], axis=dim)
    return block


def dft_table(length):
    index = jnp.arange(length, dtype=jnp.int32)
    phase = (index[:, None] * index[None, :] % length).astype(jnp.float32) * (
        2.0 * math.pi / length
    )
    cosine = jnp.cos(phase) / math.sqrt(length)
    sine = jnp.sin(phase) / math.sqrt(length)
    upper = jnp.concatenate([cosine, -sine], axis=1)
    lower = jnp.concatenate([sine, cosine], axis=1)
    return jnp.concatenate([upper, lower], axis=0).astype(jnp.bfloat16)


def share_matrix(window_half, frames):
    index = jnp.arange(frames, dtype=jnp.int32)
    inside = (jnp.abs(index[None, :] - index[:, None]) <= window_half[:, None]).astype(jnp.float32)
    return inside / jnp.sum(inside, axis=1, keepdims=True)


def adam_step(master, grad, first, second, rate):
    first_new = beta_first * first + (1.0 - beta_first) * grad
    second_new = beta_second * second + (1.0 - beta_second) * grad * grad
    first_hat = first_new / (1.0 - beta_first**STEP)
    second_hat = second_new / (1.0 - beta_second**STEP)
    master_new = master - rate * (
        first_hat / (jnp.sqrt(second_hat) + epsilon) + decay_weight * master
    )
    return (first_new, second_new, master_new)


def pad_columns(volume, margin):
    return jnp.pad(volume, ((0, 0), (0, 0), (0, 0), (0, 0), (margin, margin)))


def tap_offsets(tap_number):
    return (tap_number // 9, tap_number // 3 % 3, tap_number % 3)


def stack_taps(source, anchor, heading, extent, axis_at):
    piece_list = []
    for tap_number in range(27):
        begins = [anchor + heading * offset_one for offset_one in tap_offsets(tap_number)]
        piece_list.append(
            source[
                :,
                :,
                begins[0] : begins[0] + extent[0],
                begins[1] : begins[1] + extent[1],
                begins[2] : begins[2] + extent[2],
            ]
        )
    stacked = jnp.stack(piece_list, axis=axis_at)
    shape_now = stacked.shape
    return stacked.reshape((shape_now[0], shape_now[1] * shape_now[2]) + shape_now[3:])


def sum_taps(mixed, extent):
    summed = None
    for tap_number in range(27):
        begins = tap_offsets(tap_number)
        piece = mixed[
            :,
            tap_number,
            :,
            begins[0] : begins[0] + extent[0],
            begins[1] : begins[1] + extent[1],
            begins[2] : begins[2] + extent[2],
        ]
        summed = piece if summed is None else summed + piece
    return summed


def on_device(
    image_in,
    measured,
    target,
    line_mask,
    window_half,
    in_kernel,
    out_kernel,
    biases,
    in_moment,
    out_moment,
    bias_moment,
    in_square,
    out_square,
    bias_square,
    in_smooth,
    out_smooth,
    bias_smooth,
):
    highest = lax.Precision.HIGHEST
    slices = image_in.shape[0]
    frames_here = image_in.shape[2]
    rows_here = image_in.shape[3]
    columns = image_in.shape[4]
    frames = measured.shape[1]
    lines_here = measured.shape[2]
    width = in_kernel.shape[0]
    row_count = lax.axis_size("row")
    rows = rows_here * row_count
    batch = slices // MICRO
    table_y = dft_table(columns)
    table_x = dft_table(rows)
    share = share_matrix(window_half, frames)
    sampled_mask = line_mask.astype(jnp.float32)[None, :, :, None]
    unsampled_mask = 1.0 - sampled_mask
    count = lax.psum(jnp.sum(unsampled_mask) * (2.0 * slices * rows), ("af", "row"))
    kernel_in = in_kernel.astype(jnp.bfloat16)
    kernel_out = out_kernel.astype(jnp.bfloat16).reshape(54, width)
    bias_in = biases[:width][None, :, None, None, None]
    bias_out = biases[width:][None, :, None, None, None]
    extent = (frames_here, rows_here, columns)
    padded_extent = (frames_here + 2, rows_here + 2, columns + 2)

    def micro_step(carry, micro_index):
        start = micro_index * batch
        volume = lax.dynamic_slice_in_dim(image_in, start, batch, 0)
        observed = lax.dynamic_slice_in_dim(measured, start, batch, 0)
        wanted = lax.dynamic_slice_in_dim(target, start, batch, 0)
        volume_pad = pad_columns(with_halo(volume, (("af", 2), ("row", 3)), 1), 1)
        patches = stack_taps(volume_pad, 0, 1, extent, 2)
        preact = (
            jnp.einsum("ok,bkfxy->bofxy", kernel_in, patches, preferred_element_type=jnp.float32)
            + bias_in
        )
        hidden = jax.nn.gelu(preact).astype(jnp.bfloat16)
        hidden_pad = pad_columns(with_halo(hidden, (("af", 2), ("row", 3)), 1), 1)
        mixed = jnp.einsum(
            "kc,bcfxy->bkfxy", kernel_out, hidden_pad, preferred_element_type=jnp.float32
        )
        mixed = mixed.reshape((batch, 27, 2) + padded_extent)
        branch = sum_taps(mixed, extent) + bias_out
        image = volume.astype(jnp.float32) + branch
        rows_flat = jnp.transpose(image, (0, 2, 3, 1, 4)).reshape(
            batch, frames_here, rows_here, 2 * columns
        )
        hybrid = jnp.dot(
            rows_flat.astype(jnp.bfloat16), table_y, preferred_element_type=jnp.float32
        )
        hybrid = hybrid.astype(jnp.bfloat16).reshape(batch, frames_here, rows_here, 2, columns)
        partial_lines = lax.all_to_all(hybrid, "af", split_axis=4, concat_axis=1, tiled=True)
        spread = lax.all_to_all(partial_lines, "row", split_axis=4, concat_axis=2, tiled=True)
        spectrum = jnp.transpose(spread, (0, 1, 4, 3, 2)).reshape(
            batch, frames, lines_here, 2 * rows
        )
        kspace_data = jnp.dot(spectrum, table_x, preferred_element_type=jnp.float32)
        filled_kspace = sampled_mask * observed + unsampled_mask * kspace_data
        shared_kspace = jnp.einsum("ts,bslk->btlk", share, filled_kspace, precision=highest)
        result_image = sampled_mask * observed + unsampled_mask * shared_kspace
        differ = result_image - wanted
        root = jnp.sqrt(differ * differ + 1.0)
        loss_part = jnp.sum(unsampled_mask * (root - 1.0))
        grad_result = unsampled_mask * differ / root / count
        grad_filled = jnp.einsum(
            "ts,btlk->bslk", share, unsampled_mask * grad_result, precision=highest
        )
        grad_kspace = unsampled_mask * grad_filled
        grad_spectrum = jnp.dot(grad_kspace, table_x.T, preferred_element_type=jnp.float32).astype(
            jnp.bfloat16
        )
        grad_spread = jnp.transpose(
            grad_spectrum.reshape(batch, frames, lines_here, 2, rows), (0, 1, 4, 3, 2)
        )
        grad_partial = lax.all_to_all(grad_spread, "row", split_axis=2, concat_axis=4, tiled=True)
        grad_hybrid = lax.all_to_all(grad_partial, "af", split_axis=1, concat_axis=4, tiled=True)
        grad_rows = jnp.dot(
            grad_hybrid.reshape(batch, frames_here, rows_here, 2 * columns),
            table_y.T,
            preferred_element_type=jnp.float32,
        )
        grad_branch = jnp.transpose(
            grad_rows.reshape(batch, frames_here, rows_here, 2, columns), (0, 3, 1, 2, 4)
        ).astype(jnp.bfloat16)
        grad_pad = pad_columns(with_halo(grad_branch, (("af", 2), ("row", 3)), 1), 1)
        grad_zero = jnp.pad(grad_branch, ((0, 0), (0, 0), (2, 2), (2, 2), (2, 2)))
        grad_wide = stack_taps(grad_zero, 2, -1, padded_extent, 1)
        grad_out = jnp.einsum(
            "bkfxy,bcfxy->kc", grad_wide, hidden_pad, preferred_element_type=jnp.float32
        ).reshape(27, 2, width)
        grad_near = stack_taps(grad_pad, 2, -1, extent, 1)
        grad_hidden = jnp.einsum(
            "kc,bkfxy->bcfxy", kernel_out, grad_near, preferred_element_type=jnp.float32
        )
        gelu_back = jax.vjp(jax.nn.gelu, preact)[1]
        grad_preact = gelu_back(grad_hidden)[0].astype(jnp.bfloat16)
        grad_in = jnp.einsum(
            "bofxy,bkfxy->ok", grad_preact, patches, preferred_element_type=jnp.float32
        )
        grad_bias = jnp.concatenate(
            [
                jnp.sum(grad_preact.astype(jnp.float32), axis=(0, 2, 3, 4)),
                jnp.sum(grad_branch.astype(jnp.float32), axis=(0, 2, 3, 4)),
            ]
        )
        return (
            (carry[0] + grad_in, carry[1] + grad_out, carry[2] + grad_bias, carry[3] + loss_part),
            None,
        )

    initial = (
        jnp.zeros_like(in_kernel),
        jnp.zeros_like(out_kernel),
        jnp.zeros_like(biases),
        jnp.zeros((), jnp.float32),
    )
    totals = lax.scan(micro_step, initial, jnp.arange(MICRO, dtype=jnp.int32))[0]
    grad_in, grad_out, grad_bias, loss_total = totals
    grad_in, grad_out, grad_bias, loss_total = lax.psum(
        (grad_in, grad_out, grad_bias, loss_total), ("af", "row")
    )
    in_first, in_second, in_master = adam_step(in_kernel, grad_in, in_moment, in_square, rate_in)
    out_first, out_second, out_master = adam_step(
        out_kernel, grad_out, out_moment, out_square, rate_out
    )
    bias_first, bias_second, bias_master = adam_step(
        biases, grad_bias, bias_moment, bias_square, rate_bias
    )
    in_average = average_keep * in_smooth + (1.0 - average_keep) * in_master
    out_average = average_keep * out_smooth + (1.0 - average_keep) * out_master
    bias_average = average_keep * bias_smooth + (1.0 - average_keep) * bias_master
    return (
        loss_total,
        count,
        in_first,
        out_first,
        bias_first,
        in_second,
        out_second,
        bias_second,
        in_master,
        out_master,
        bias_master,
        in_average,
        out_average,
        bias_average,
        in_master.astype(jnp.bfloat16),
        out_master.astype(jnp.bfloat16),
        bias_master.astype(jnp.bfloat16),
    )


def solution(mesh):
    in_specs = (
        P(None, None, "af", "row", None),
        P(None, None, ("af", "row"), None),
        P(None, None, ("af", "row"), None),
        P(None, ("af", "row")),
        P(),
        P(),
        P(),
        P(),
        P(),
        P(),
        P(),
        P(),
        P(),
        P(),
        P(),
        P(),
        P(),
    )
    out_specs = (
        P(),
        P(),
        P(),
        P(),
        P(),
        P(),
        P(),
        P(),
        P(),
        P(),
        P(),
        P(),
        P(),
        P(),
        P(),
        P(),
        P(),
    )
    return jax.shard_map(
        on_device, mesh=mesh, in_specs=in_specs, out_specs=out_specs, check_vma=False
    )
```

profile of v0, /device:TPU:0, one launch (start us, length us, event | category | flops | bytes accessed | tf_op | source)
XLA Modules:
  0.0 2619.5 jit_solution(16642739411341635534)
XLA Ops:
  2.7 42.0 %psum.35 = f32[]{:T(128)} all-reduce(f32[]{:T(128)S(6)} %mul.368), channel_id=1, replica_groups=mesh['af'=4,'row'=8] {'af','row'}, use_global_device_ids=true, to_apply=%region_2.3 | all-reduce | flops 1 | bytes 8 | tf_op jit(solution)/shard_map/psum | solution.py:141
  51.9 2521.9 %while.20 = (s32[]{:T(128)}, f32[64,54]{0,1:T(8,128)}, f32[27,2,64]{2,0,1:T(8,128)S(1)}, f32[66]{0:T(128)}, f32[]{:T(128)}, /*index=5*/f32[1,20,8,1]{2,1,3,0:T(8...) while((s32[]{:T(128)}, f32[64,54]{0,1:T(8,128)}, ...), condition=%wide.region_7.8_spmd.clone, body=%wide.region_3.7_spmd.clone.sunk | while | flops 2315546624 | bytes 312050304 | solution.py:240
  133.1 22.3 copy.746
  335.4 21.8 collective-permute-done.4
  380.2 22.3 copy.746
  582.8 21.8 collective-permute-done.4
  627.7 22.3 copy.746
  669.5 24.5 all_to_all.140
  841.7 21.8 collective-permute-done.4
  886.6 22.3 copy.746
  1134.0 22.3 copy.746
  1175.9 24.5 all_to_all.140
  1348.1 21.8 collective-permute-done.4
  1393.0 22.3 copy.746
  1640.4 22.3 copy.746
  1682.2 24.5 all_to_all.140
  1854.5 21.8 collective-permute-done.4
  1899.3 22.3 copy.746
  2101.9 21.8 collective-permute-done.4
  2146.8 22.3 copy.746
  2188.6 24.5 all_to_all.140
  2360.8 21.8 collective-permute-done.4
  2405.7 22.3 copy.746
  2573.8 41.8 %all-reduce.4 = (f32[]{:T(128)}, f32[64,54]{0,1:T(8,128)S(1)}, f32[27,2,64]{2,1,0:T(2,128)S(1)}, f32[66]{0:T(128)S(1)}) all-reduce(f32[]{:T(128)} %get-tuple-element.285, f32[64,54]{0,1:T(8,128)} %get-tuple-element.286, f32[27,2,64]{2,1,0:T(2,128)S(1)} %copy.442, f32[66]{0:T(128)} %get-tuple-element.288), channel_id=1, replica_groups=mesh['af'=4,'row'=8] {'af','row'}, use_global_device_ids=true, to_apply=%region_8.9 | all-reduce | flops 6979 | bytes 55832 | tf_op jit(solution)/shard_map/psum | solution.py:242
  (2062 shorter events, 2017.4 us)
Async XLA Ops:
  81.9 27.0 %collective-permute-start.4 = (bf16[1,64,1,32,256]{4,1,3,2,0:T(8,128)(2,1)S(1)}, bf16[1,64,1,32,256]{4,1,3,2,0:T(8,128)(2,1)S(1)}, u32[]{:S(2)}, u32[]{:S(2)}) collective-permute-start(bf16[1,64,1,32,256]{4,1,3,2,0:T(8,128)(2,1)S(1)} %get-tuple-element.655), channel_id=1, source_target_pairs={{8,0},{16,8},{24,16},{9,1},{17,9},{25,17},{10,2},{18,10},{26,18},{... | collective-permute-start | bytes 3145736 | tf_op jit(solution)/shard_map/while/body/eval_jaxpr/ppermute | solution.py:30
  83.2 27.5 %collective-permute-start.5 = (bf16[1,64,1,32,256]{4,1,3,2,0:T(8,128)(2,1)S(1)}, bf16[1,64,1,32,256]{4,1,3,2,0:T(8,128)(2,1)S(1)}, u32[]{:S(2)}, u32[]{:S(2)}) collective-permute-start(bf16[1,64,1,32,256]{4,1,3,2,0:T(8,128)(2,1)S(1)} %get-tuple-element.656), channel_id=1, source_target_pairs={{0,8},{8,16},{16,24},{1,9},{9,17},{17,25},{2,10},{10,18},{18,26},{... | collective-permute-start | bytes 3145736 | tf_op jit(solution)/shard_map/while/body/eval_jaxpr/ppermute | solution.py:27
  251.5 23.7 collective-permute-start.10
  329.1 28.1 %collective-permute-start.4 = (bf16[1,64,1,32,256]{4,1,3,2,0:T(8,128)(2,1)S(1)}, bf16[1,64,1,32,256]{4,1,3,2,0:T(8,128)(2,1)S(1)}, u32[]{:S(2)}, u32[]{:S(2)}) collective-permute-start(bf16[1,64,1,32,256]{4,1,3,2,0:T(8,128)(2,1)S(1)} %get-tuple-element.655), channel_id=1, source_target_pairs={{8,0},{16,8},{24,16},{9,1},{17,9},{25,17},{10,2},{18,10},{26,18},{... | collective-permute-start | bytes 3145736 | tf_op jit(solution)/shard_map/while/body/eval_jaxpr/ppermute | solution.py:30
  330.4 27.9 %collective-permute-start.5 = (bf16[1,64,1,32,256]{4,1,3,2,0:T(8,128)(2,1)S(1)}, bf16[1,64,1,32,256]{4,1,3,2,0:T(8,128)(2,1)S(1)}, u32[]{:S(2)}, u32[]{:S(2)}) collective-permute-start(bf16[1,64,1,32,256]{4,1,3,2,0:T(8,128)(2,1)S(1)} %get-tuple-element.656), channel_id=1, source_target_pairs={{0,8},{8,16},{16,24},{1,9},{9,17},{17,25},{2,10},{10,18},{18,26},{... | collective-permute-start | bytes 3145736 | tf_op jit(solution)/shard_map/while/body/eval_jaxpr/ppermute | solution.py:27
  576.6 28.1 %collective-permute-start.4 = (bf16[1,64,1,32,256]{4,1,3,2,0:T(8,128)(2,1)S(1)}, bf16[1,64,1,32,256]{4,1,3,2,0:T(8,128)(2,1)S(1)}, u32[]{:S(2)}, u32[]{:S(2)}) collective-permute-start(bf16[1,64,1,32,256]{4,1,3,2,0:T(8,128)(2,1)S(1)} %get-tuple-element.655), channel_id=1, source_target_pairs={{8,0},{16,8},{24,16},{9,1},{17,9},{25,17},{10,2},{18,10},{26,18},{... | collective-permute-start | bytes 3145736 | tf_op jit(solution)/shard_map/while/body/eval_jaxpr/ppermute | solution.py:30
  577.9 27.9 %collective-permute-start.5 = (bf16[1,64,1,32,256]{4,1,3,2,0:T(8,128)(2,1)S(1)}, bf16[1,64,1,32,256]{4,1,3,2,0:T(8,128)(2,1)S(1)}, u32[]{:S(2)}, u32[]{:S(2)}) collective-permute-start(bf16[1,64,1,32,256]{4,1,3,2,0:T(8,128)(2,1)S(1)} %get-tuple-element.656), channel_id=1, source_target_pairs={{0,8},{8,16},{16,24},{1,9},{9,17},{17,25},{2,10},{10,18},{18,26},{... | collective-permute-start | bytes 3145736 | tf_op jit(solution)/shard_map/while/body/eval_jaxpr/ppermute | solution.py:27
  757.9 23.7 collective-permute-start.10
  835.5 28.1 %collective-permute-start.4 = (bf16[1,64,1,32,256]{4,1,3,2,0:T(8,128)(2,1)S(1)}, bf16[1,64,1,32,256]{4,1,3,2,0:T(8,128)(2,1)S(1)}, u32[]{:S(2)}, u32[]{:S(2)}) collective-permute-start(bf16[1,64,1,32,256]{4,1,3,2,0:T(8,128)(2,1)S(1)} %get-tuple-element.655), channel_id=1, source_target_pairs={{8,0},{16,8},{24,16},{9,1},{17,9},{25,17},{10,2},{18,10},{26,18},{... | collective-permute-start | bytes 3145736 | tf_op jit(solution)/shard_map/while/body/eval_jaxpr/ppermute | solution.py:30
  836.8 27.9 %collective-permute-start.5 = (bf16[1,64,1,32,256]{4,1,3,2,0:T(8,128)(2,1)S(1)}, bf16[1,64,1,32,256]{4,1,3,2,0:T(8,128)(2,1)S(1)}, u32[]{:S(2)}, u32[]{:S(2)}) collective-permute-start(bf16[1,64,1,32,256]{4,1,3,2,0:T(8,128)(2,1)S(1)} %get-tuple-element.656), channel_id=1, source_target_pairs={{0,8},{8,16},{16,24},{1,9},{9,17},{17,25},{2,10},{10,18},{18,26},{... | collective-permute-start | bytes 3145736 | tf_op jit(solution)/shard_map/while/body/eval_jaxpr/ppermute | solution.py:27
  1083.0 28.1 %collective-permute-start.4 = (bf16[1,64,1,32,256]{4,1,3,2,0:T(8,128)(2,1)S(1)}, bf16[1,64,1,32,256]{4,1,3,2,0:T(8,128)(2,1)S(1)}, u32[]{:S(2)}, u32[]{:S(2)}) collective-permute-start(bf16[1,64,1,32,256]{4,1,3,2,0:T(8,128)(2,1)S(1)} %get-tuple-element.655), channel_id=1, source_target_pairs={{8,0},{16,8},{24,16},{9,1},{17,9},{25,17},{10,2},{18,10},{26,18},{... | collective-permute-start | bytes 3145736 | tf_op jit(solution)/shard_map/while/body/eval_jaxpr/ppermute | solution.py:30
  1084.3 27.9 %collective-permute-start.5 = (bf16[1,64,1,32,256]{4,1,3,2,0:T(8,128)(2,1)S(1)}, bf16[1,64,1,32,256]{4,1,3,2,0:T(8,128)(2,1)S(1)}, u32[]{:S(2)}, u32[]{:S(2)}) collective-permute-start(bf16[1,64,1,32,256]{4,1,3,2,0:T(8,128)(2,1)S(1)} %get-tuple-element.656), channel_id=1, source_target_pairs={{0,8},{8,16},{16,24},{1,9},{9,17},{17,25},{2,10},{10,18},{18,26},{... | collective-permute-start | bytes 3145736 | tf_op jit(solution)/shard_map/while/body/eval_jaxpr/ppermute | solution.py:27
  1264.3 23.7 collective-permute-start.10
  1341.9 28.1 %collective-permute-start.4 = (bf16[1,64,1,32,256]{4,1,3,2,0:T(8,128)(2,1)S(1)}, bf16[1,64,1,32,256]{4,1,3,2,0:T(8,128)(2,1)S(1)}, u32[]{:S(2)}, u32[]{:S(2)}) collective-permute-start(bf16[1,64,1,32,256]{4,1,3,2,0:T(8,128)(2,1)S(1)} %get-tuple-element.655), channel_id=1, source_target_pairs={{8,0},{16,8},{24,16},{9,1},{17,9},{25,17},{10,2},{18,10},{26,18},{... | collective-permute-start | bytes 3145736 | tf_op jit(solution)/shard_map/while/body/eval_jaxpr/ppermute | solution.py:30
  1343.2 27.9 %collective-permute-start.5 = (bf16[1,64,1,32,256]{4,1,3,2,0:T(8,128)(2,1)S(1)}, bf16[1,64,1,32,256]{4,1,3,2,0:T(8,128)(2,1)S(1)}, u32[]{:S(2)}, u32[]{:S(2)}) collective-permute-start(bf16[1,64,1,32,256]{4,1,3,2,0:T(8,128)(2,1)S(1)} %get-tuple-element.656), channel_id=1, source_target_pairs={{0,8},{8,16},{16,24},{1,9},{9,17},{17,25},{2,10},{10,18},{18,26},{... | collective-permute-start | bytes 3145736 | tf_op jit(solution)/shard_map/while/body/eval_jaxpr/ppermute | solution.py:27
  1589.3 28.1 %collective-permute-start.4 = (bf16[1,64,1,32,256]{4,1,3,2,0:T(8,128)(2,1)S(1)}, bf16[1,64,1,32,256]{4,1,3,2,0:T(8,128)(2,1)S(1)}, u32[]{:S(2)}, u32[]{:S(2)}) collective-permute-start(bf16[1,64,1,32,256]{4,1,3,2,0:T(8,128)(2,1)S(1)} %get-tuple-element.655), channel_id=1, source_target_pairs={{8,0},{16,8},{24,16},{9,1},{17,9},{25,17},{10,2},{18,10},{26,18},{... | collective-permute-start | bytes 3145736 | tf_op jit(solution)/shard_map/while/body/eval_jaxpr/ppermute | solution.py:30
  1590.6 27.9 %collective-permute-start.5 = (bf16[1,64,1,32,256]{4,1,3,2,0:T(8,128)(2,1)S(1)}, bf16[1,64,1,32,256]{4,1,3,2,0:T(8,128)(2,1)S(1)}, u32[]{:S(2)}, u32[]{:S(2)}) collective-permute-start(bf16[1,64,1,32,256]{4,1,3,2,0:T(8,128)(2,1)S(1)} %get-tuple-element.656), channel_id=1, source_target_pairs={{0,8},{8,16},{16,24},{1,9},{9,17},{17,25},{2,10},{10,18},{18,26},{... | collective-permute-start | bytes 3145736 | tf_op jit(solution)/shard_map/while/body/eval_jaxpr/ppermute | solution.py:27
  1770.6 23.7 collective-permute-start.10
  1848.2 28.1 %collective-permute-start.4 = (bf16[1,64,1,32,256]{4,1,3,2,0:T(8,128)(2,1)S(1)}, bf16[1,64,1,32,256]{4,1,3,2,0:T(8,128)(2,1)S(1)}, u32[]{:S(2)}, u32[]{:S(2)}) collective-permute-start(bf16[1,64,1,32,256]{4,1,3,2,0:T(8,128)(2,1)S(1)} %get-tuple-element.655), channel_id=1, source_target_pairs={{8,0},{16,8},{24,16},{9,1},{17,9},{25,17},{10,2},{18,10},{26,18},{... | collective-permute-start | bytes 3145736 | tf_op jit(solution)/shard_map/while/body/eval_jaxpr/ppermute | solution.py:30
  1849.5 27.9 %collective-permute-start.5 = (bf16[1,64,1,32,256]{4,1,3,2,0:T(8,128)(2,1)S(1)}, bf16[1,64,1,32,256]{4,1,3,2,0:T(8,128)(2,1)S(1)}, u32[]{:S(2)}, u32[]{:S(2)}) collective-permute-start(bf16[1,64,1,32,256]{4,1,3,2,0:T(8,128)(2,1)S(1)} %get-tuple-element.656), channel_id=1, source_target_pairs={{0,8},{8,16},{16,24},{1,9},{9,17},{17,25},{2,10},{10,18},{18,26},{... | collective-permute-start | bytes 3145736 | tf_op jit(solution)/shard_map/while/body/eval_jaxpr/ppermute | solution.py:27
  2095.7 28.1 %collective-permute-start.4 = (bf16[1,64,1,32,256]{4,1,3,2,0:T(8,128)(2,1)S(1)}, bf16[1,64,1,32,256]{4,1,3,2,0:T(8,128)(2,1)S(1)}, u32[]{:S(2)}, u32[]{:S(2)}) collective-permute-start(bf16[1,64,1,32,256]{4,1,3,2,0:T(8,128)(2,1)S(1)} %get-tuple-element.655), channel_id=1, source_target_pairs={{8,0},{16,8},{24,16},{9,1},{17,9},{25,17},{10,2},{18,10},{26,18},{... | collective-permute-start | bytes 3145736 | tf_op jit(solution)/shard_map/while/body/eval_jaxpr/ppermute | solution.py:30
  2097.0 27.9 %collective-permute-start.5 = (bf16[1,64,1,32,256]{4,1,3,2,0:T(8,128)(2,1)S(1)}, bf16[1,64,1,32,256]{4,1,3,2,0:T(8,128)(2,1)S(1)}, u32[]{:S(2)}, u32[]{:S(2)}) collective-permute-start(bf16[1,64,1,32,256]{4,1,3,2,0:T(8,128)(2,1)S(1)} %get-tuple-element.656), channel_id=1, source_target_pairs={{0,8},{8,16},{16,24},{1,9},{9,17},{17,25},{2,10},{10,18},{18,26},{... | collective-permute-start | bytes 3145736 | tf_op jit(solution)/shard_map/while/body/eval_jaxpr/ppermute | solution.py:27
  2354.6 28.1 %collective-permute-start.4 = (bf16[1,64,1,32,256]{4,1,3,2,0:T(8,128)(2,1)S(1)}, bf16[1,64,1,32,256]{4,1,3,2,0:T(8,128)(2,1)S(1)}, u32[]{:S(2)}, u32[]{:S(2)}) collective-permute-start(bf16[1,64,1,32,256]{4,1,3,2,0:T(8,128)(2,1)S(1)} %get-tuple-element.655), channel_id=1, source_target_pairs={{8,0},{16,8},{24,16},{9,1},{17,9},{25,17},{10,2},{18,10},{26,18},{... | collective-permute-start | bytes 3145736 | tf_op jit(solution)/shard_map/while/body/eval_jaxpr/ppermute | solution.py:30
  2355.9 27.9 %collective-permute-start.5 = (bf16[1,64,1,32,256]{4,1,3,2,0:T(8,128)(2,1)S(1)}, bf16[1,64,1,32,256]{4,1,3,2,0:T(8,128)(2,1)S(1)}, u32[]{:S(2)}, u32[]{:S(2)}) collective-permute-start(bf16[1,64,1,32,256]{4,1,3,2,0:T(8,128)(2,1)S(1)} %get-tuple-element.656), channel_id=1, source_target_pairs={{0,8},{8,16},{16,24},{1,9},{9,17},{17,25},{2,10},{10,18},{18,26},{... | collective-permute-start | bytes 3145736 | tf_op jit(solution)/shard_map/while/body/eval_jaxpr/ppermute | solution.py:27
  (291 other events, 33903.7 us)
where the time goes:
time: 2630 us; the launch traced here: 2620 us
  local copies, waits for them, and re-layouts  674 us (26%)
  matrix products  674 us (26%)
  blocking collectives  486 us (18%)
  starting transfers between devices  350 us (13%)
  waiting for transfers between devices  323 us (12%)
  other arithmetic  69.1 us (3%)
  loops' own time  42.7 us (2%)
    ppermute x60, starting transfers between devices, with_halo(): lax.ppermute(lax.slice_in_dim(block, block.shape[dim] - width, None, axis...  239 us
    transpose x10, local copies, waits for them, and re-layouts, micro_step(): jnp.einsum('kc,bcfxy->bkfxy', kernel_out, hidden_pad, preferred_element_t...  223 us
    ppermute x60, waiting for transfers between devices, with_halo(): lax.ppermute(lax.slice_in_dim(block, 0, width, axis=dim), axis, backward)  217 us
    dot_general x10, matrix products, micro_step(): jnp.einsum('bkfxy,bcfxy->kc', grad_wide, hidden_pad, preferred_element_ty...  191 us
    all_to_all x10, blocking collectives, micro_step(): lax.all_to_all(hybrid, 'af', split_axis=4, concat_axis=1, tiled=True)  177 us
    while x1170, local copies, waits for them, and re-layouts  174 us
    dot_general x10, matrix products, micro_step(): jnp.einsum('kc,bkfxy->bcfxy', kernel_out, grad_near, preferred_element_ty...  165 us
    dot_general x10, matrix products, micro_step(): jnp.einsum('kc,bcfxy->bkfxy', kernel_out, hidden_pad, preferred_element_t...  156 us
  transfers between devices with their start and end apart: 130, of which 70 were waited for; matrix products, arithmetic and copies ran while one was open for 8% of the time, Pallas kernels for 0%

commit v1 on v0

v1 whole, which is shorter than its diff:
```python
import functools
import math

import jax
import jax.numpy as jnp
import numpy as np
from jax import lax
from jax.experimental import pallas as pl
from jax.experimental.pallas import tpu as pltpu
from jax.sharding import PartitionSpec as P

STEP = 5
AXES = ("af", "row")
BLOCK = 4
WIN = 8
SIDE = 16
DEPTH = 9 * SIDE
ONES_ROW = BLOCK + 2
VMEM = 60 * 2**20
GELU = math.sqrt(2.0 / math.pi)
CUBE = 0.044715

beta_first = 0.5
beta_second = 0.5
rate_in = 0.2
rate_out = 0.04
rate_bias = 0.3
decay_weight = 0.01
average_keep = 0.9
epsilon = 1e-08

NT = (((1,), (1,)), ((), ()))
TN = (((0,), (0,)), ((), ()))


def dft_table(length):
    index = np.arange(length)
    phase = (index[:, None] * index[None, :] % length) * (2.0 * math.pi / length)
    cosine = np.cos(phase) / math.sqrt(length)
    sine = np.sin(phase) / math.sqrt(length)
    upper = np.concatenate([cosine, -sine], axis=1)
    lower = np.concatenate([sine, cosine], axis=1)
    return np.concatenate([upper, lower], axis=0).astype(np.float32)


def share_matrix(window_half, frames):
    index = jnp.arange(frames, dtype=jnp.int32)
    inside = (jnp.abs(index[None, :] - index[:, None]) <= window_half[:, None]).astype(jnp.float32)
    return inside / jnp.sum(inside, axis=1, keepdims=True)


def adam_step(master, grad, first, second, rate):
    first_new = beta_first * first + (1.0 - beta_first) * grad
    second_new = beta_second * second + (1.0 - beta_second) * grad * grad
    first_hat = first_new / (1.0 - beta_first**STEP)
    second_hat = second_new / (1.0 - beta_second**STEP)
    master_new = master - rate * (
        first_hat / (jnp.sqrt(second_hat) + epsilon) + decay_weight * master
    )
    return (first_new, second_new, master_new)


def conv_in_weights(kernel, bias):
    width = kernel.shape[0]
    taps = kernel.astype(jnp.bfloat16).astype(jnp.float32).reshape(width, 2, 3, 3, 3)
    rows = []
    for j in range(BLOCK):
        row = jnp.pad(taps, ((0, 0), (0, 0), (0, 0), (j, WIN - 3 - j), (0, 0)))
        rows.append(row.transpose(0, 2, 4, 1, 3))
    spread = jnp.stack(rows)
    high = lax.reduce_precision(bias, 8, 7)
    rest = bias - high
    middle = lax.reduce_precision(rest, 8, 7)
    parts = jnp.stack([high, middle, rest - middle], axis=1)
    spread = spread.at[:, :, :, 0, 0, ONES_ROW].set(jnp.broadcast_to(parts, (BLOCK, width, 3)))
    return spread.reshape(BLOCK * width, DEPTH).astype(jnp.bfloat16)


def conv_out_weights(kernel):
    width = kernel.shape[2]
    taps = kernel.astype(jnp.bfloat16).reshape(3, 3, 3, 2, width)[:, ::-1]
    columns = []
    for j in range(BLOCK):
        column = jnp.pad(taps, ((0, 0), (j, WIN - 3 - j), (0, 0), (0, 0), (0, 0)))
        columns.append(column.transpose(0, 2, 3, 1, 4))
    return jnp.stack(columns, axis=4).reshape(DEPTH, BLOCK * width)


def conv_back_weights(kernel):
    width = kernel.shape[2]
    taps = kernel.astype(jnp.bfloat16).reshape(3, 3, 3, 2, width)[::-1, ::-1, ::-1]
    rows = []
    for j in range(BLOCK):
        row = jnp.pad(taps, ((0, 0), (j, WIN - 3 - j), (0, 0), (0, 0), (0, 0)))
        rows.append(row.transpose(4, 0, 2, 3, 1))
    return jnp.stack(rows).reshape(BLOCK * width, DEPTH)


def fold_in(total, width):
    spread = total.reshape(BLOCK, width, 3, 3, 2, WIN)
    taps = sum(spread[j][..., j : j + 3] for j in range(BLOCK))
    grad = taps.transpose(0, 3, 1, 4, 2).reshape(width, 54)
    return grad, jnp.sum(spread[:, :, 0, 0, 0, ONES_ROW], axis=0)


def fold_out(total, width):
    spread = total.reshape(BLOCK, width, 3, 3, 2, WIN)
    taps = sum(spread[j][..., j : j + 3] for j in range(BLOCK))
    return taps[:, ::-1, ::-1, :, ::-1].transpose(1, 4, 2, 3, 0).reshape(27, 2, width)


def load_volume(volume, own, edge_frames, edge_rows):
    _, channels, frames, rows, columns = own.shape
    lanes = (frames + 2) * columns
    for c in range(channels):
        volume[c, rows + 8 : rows + 16, :] = jnp.zeros((8, lanes), jnp.float32)
        for t in range(frames + 2):
            if t == 0:
                piece = edge_frames[0, 0, c]
            elif t == frames + 1:
                piece = edge_frames[0, 1, c]
            else:
                piece = own[0, c, t - 1]
            volume[c, 8 : 8 + rows, t * columns : (t + 1) * columns] = piece.astype(jnp.float32)
    outer = edge_rows[0].astype(jnp.float32)
    for c in range(channels):
        volume[c, 7:8, :] = outer[c : c + 1]
        volume[c, rows + 8 : rows + 9, :] = outer[2 + c : 3 + c]


def build_windows(volume, windows, columns, ones):
    blocks, _, lanes = windows.shape
    column = lax.broadcasted_iota(jnp.int32, (SIDE, columns), 1)
    row = lax.broadcasted_iota(jnp.int32, (SIDE, columns), 0)
    for block in range(blocks):
        for t in range(lanes // columns):
            here = slice(t * columns, (t + 1) * columns)
            start = 7 + BLOCK * block
            window = jnp.concatenate(
                [volume[c, start : start + WIN, here] for c in range(2)], axis=0
            )
            for e in range(3):
                shifted = window
                if e != 1:
                    shifted = pltpu.roll(window, (1 - e) % columns, axis=1)
                    shifted = jnp.where(column == (0 if e == 0 else columns - 1), 0.0, shifted)
                if ones and e == 0:
                    shifted = jnp.where(row == ONES_ROW, 1.0, shifted)
                windows[block, e * SIDE : (e + 1) * SIDE, here] = shifted.astype(jnp.bfloat16)


def forward_kernel(
    own, edge_frames, edge_rows, w_in, w_out, bias_out, main, part_frames, part_rows,
    volume, windows, total, hidden, mixed, spread,
):
    _, _, frames, rows, columns = own.shape
    blocks = windows.shape[0]
    load_volume(volume, own, edge_frames, edge_rows)
    build_windows(volume, windows, columns, True)
    column = lax.broadcasted_iota(jnp.int32, (SIDE, columns), 1)

    def step(block, carry):
        for f in range(frames):
            here = slice(f * columns, (f + 1) * columns)
            patch = jnp.concatenate(
                [windows[block, :, (f + a) * columns : (f + a + 1) * columns] for a in range(3)],
                axis=0,
            )
            x = jnp.dot(w_in[...], patch, preferred_element_type=jnp.float32)
            t = jnp.tanh(x * (GELU + (GELU * CUBE) * (x * x)))
            half = 0.5 * x
            hidden[:, here] = (half + half * t).astype(jnp.bfloat16)
            mixed[f] = jnp.dot(w_out[...], hidden[:, here], preferred_element_type=jnp.float32)
        for t in range(frames + 2):
            window = None
            for e in range(3):
                summed = None
                for a in range(3):
                    f = t - 2 + a
                    if 0 <= f < frames:
                        start = (a * 3 + e) * SIDE
                        piece = mixed[f, start : start + SIDE, :]
                        summed = piece if summed is None else summed + piece
                if e != 1:
                    summed = pltpu.roll(summed, (1 - e) % columns, axis=1)
                    summed = jnp.where(column == (0 if e == 0 else columns - 1), 0.0, summed)
                window = summed if window is None else window + summed
            spread[block, :, t * columns : (t + 1) * columns] = window
        return carry

    lax.fori_loop(0, blocks, step, 0)
    total[...] = jnp.zeros_like(total)
    for block in range(blocks):
        for o in range(2):
            start = 7 + BLOCK * block
            total[o, start : start + WIN, :] = (
                total[o, start : start + WIN, :] + spread[block, o * WIN : (o + 1) * WIN, :]
            )
    for o in range(2):
        for t in range(frames + 2):
            here = total[o, 8 : 8 + rows, t * columns : (t + 1) * columns]
            if t == 0:
                part_frames[0, 0, o] = here.astype(jnp.bfloat16)
            elif t == frames + 1:
                part_frames[0, 1, o] = here.astype(jnp.bfloat16)
            else:
                base = volume[o, 8 : 8 + rows, t * columns : (t + 1) * columns] + bias_out[o]
                main[0, t - 1, :, o * columns : (o + 1) * columns] = base + here
    part_rows[0] = jnp.concatenate(
        [total[o, at : at + 1, :] for at in (7, 8 + rows) for o in range(2)], axis=0
    ).astype(jnp.bfloat16)


def backward_kernel(
    own, edge_frames, edge_rows, grad, grad_frames, grad_rows, w_in, w_back, sum_in, sum_out,
    volume, windows, grad_windows, hidden, grads,
):
    _, _, frames, rows, columns = own.shape
    blocks = windows.shape[0]

    @pl.when(pl.program_id(0) == 0)
    def _():
        sum_in[...] = jnp.zeros_like(sum_in)
        sum_out[...] = jnp.zeros_like(sum_out)

    load_volume(volume, own, edge_frames, edge_rows)
    build_windows(volume, windows, columns, True)
    load_volume(volume, grad, grad_frames, grad_rows)
    build_windows(volume, grad_windows, columns, False)

    def step(block, carry):
        def patches(source):
            return jnp.concatenate(
                [source[block, :, a * columns : (a + frames) * columns] for a in range(3)], axis=0
            )

        patch = patches(windows)
        grad_patch = patches(grad_windows)
        for f in range(frames):
            here = slice(f * columns, (f + 1) * columns)
            x = jnp.dot(w_in[...], patch[:, here], preferred_element_type=jnp.float32)
            gh = jnp.dot(w_back[...], grad_patch[:, here], preferred_element_type=jnp.float32)
            u = x * x
            t = jnp.tanh(x * (GELU + (GELU * CUBE) * u))
            gate = 0.5 + 0.5 * t
            hidden[:, here] = (x * gate).astype(jnp.bfloat16)
            slope = x * (2.0 * GELU + (6.0 * GELU * CUBE) * u)
            grads[:, here] = (gate * (1.0 + slope * (1.0 - gate)) * gh).astype(jnp.bfloat16)
        sum_in[...] += lax.dot_general(grads[...], patch, NT, preferred_element_type=jnp.float32)
        sum_out[...] += lax.dot_general(
            hidden[...], grad_patch, NT, preferred_element_type=jnp.float32
        )
        return carry

    lax.fori_loop(0, blocks, step, 0)


def whole(shape):
    return pl.BlockSpec(tuple(shape), lambda s: (0,) * len(shape))


def a_slice(shape):
    return pl.BlockSpec((1,) + tuple(shape[1:]), lambda s: (s,) + (0,) * (len(shape) - 1))


def conv_scratch(frames, rows, columns):
    lanes = (frames + 2) * columns
    return (
        pltpu.VMEM((2, rows + 16, lanes), jnp.float32),
        pltpu.VMEM((rows // BLOCK, 3 * SIDE, lanes), jnp.bfloat16),
    )


def conv_forward(own, edge_frames, edge_rows, w_in, w_out, bias_out):
    slices, _, frames, rows, columns = own.shape
    lanes = (frames + 2) * columns
    span = w_in.shape[0]
    volume, windows = conv_scratch(frames, rows, columns)
    out_shape = [
        jax.ShapeDtypeStruct((slices, frames, rows, 2 * columns), jnp.float32),
        jax.ShapeDtypeStruct((slices, 2, 2, rows, columns), jnp.bfloat16),
        jax.ShapeDtypeStruct((slices, 4, lanes), jnp.bfloat16),
    ]
    return pl.pallas_call(
        forward_kernel,
        grid=(slices,),
        in_specs=[
            a_slice(own.shape),
            a_slice(edge_frames.shape),
            a_slice(edge_rows.shape),
            whole(w_in.shape),
            whole(w_out.shape),
            pl.BlockSpec(memory_space=pltpu.SMEM),
        ],
        out_specs=[a_slice(one.shape) for one in out_shape],
        out_shape=out_shape,
        scratch_shapes=[
            volume,
            windows,
            volume,
            pltpu.VMEM((span, frames * columns), jnp.bfloat16),
            pltpu.VMEM((frames, DEPTH, columns), jnp.float32),
            pltpu.VMEM((rows // BLOCK, SIDE, lanes), jnp.float32),
        ],
        compiler_params=pltpu.CompilerParams(vmem_limit_bytes=VMEM),
        name="conv_forward",
    )(own, edge_frames, edge_rows, w_in, w_out, bias_out)


def conv_backward(own, edge_frames, edge_rows, grad, grad_frames, grad_rows, w_in, w_back):
    slices, _, frames, rows, columns = own.shape
    span = w_in.shape[0]
    volume, windows = conv_scratch(frames, rows, columns)
    halves = pltpu.VMEM((span, frames * columns), jnp.bfloat16)
    total = jax.ShapeDtypeStruct((span, DEPTH), jnp.float32)
    arrays = (own, edge_frames, edge_rows, grad, grad_frames, grad_rows)
    return pl.pallas_call(
        backward_kernel,
        grid=(slices,),
        in_specs=[a_slice(one.shape) for one in arrays] + [whole(w_in.shape), whole(w_back.shape)],
        out_specs=[whole(total.shape)] * 2,
        out_shape=[total] * 2,
        scratch_shapes=[volume, windows, windows, halves, halves],
        compiler_params=pltpu.CompilerParams(vmem_limit_bytes=VMEM),
        name="conv_backward",
    )(*arrays, w_in, w_back)


def along(axis, step):
    count = lax.axis_size(axis)
    return [(i, i + step) for i in range(count) if 0 <= i + step < count]


def edges_of(volume):
    slices, _, frames, rows, columns = volume.shape
    below = lax.ppermute(volume[:, :, frames - 1], "af", along("af", 1))
    above = lax.ppermute(volume[:, :, 0], "af", along("af", -1))
    edge_frames = jnp.stack([below, above], axis=1)

    def flat(at):
        middle = volume[:, :, :, at].reshape(slices, 2, frames * columns)
        return jnp.concatenate([below[:, :, at], middle, above[:, :, at]], axis=2)

    left = lax.ppermute(flat(rows - 1), "row", along("row", 1))
    right = lax.ppermute(flat(0), "row", along("row", -1))
    return edge_frames, jnp.concatenate([left, right], axis=1)


def return_edges(part_frames, part_rows, columns):
    to_below = lax.ppermute(part_frames[:, 0], "af", along("af", -1))
    to_above = lax.ppermute(part_frames[:, 1], "af", along("af", 1))
    first = lax.ppermute(part_rows[:, :, :columns], "af", along("af", -1))
    last = lax.ppermute(part_rows[:, :, -columns:], "af", along("af", 1))
    frames = part_rows.shape[2] // columns - 2
    middle = part_rows[:, :, columns:-columns].astype(jnp.float32)
    wide = (frames - 1) * columns
    middle = middle + jnp.pad(first.astype(jnp.float32), ((0, 0), (0, 0), (wide, 0)))
    middle = middle + jnp.pad(last.astype(jnp.float32), ((0, 0), (0, 0), (0, wide)))
    middle = middle.astype(jnp.bfloat16)
    lower = lax.ppermute(middle[:, 0:2], "row", along("row", -1))
    upper = lax.ppermute(middle[:, 2:4], "row", along("row", 1))
    return jnp.stack([to_above, to_below], axis=1), jnp.concatenate([upper, lower], axis=1)


def image_kernel(main, add_frames, add_rows, table, out, image):
    slices, frames, rows, twice = main.shape
    columns = twice // 2
    row = lax.broadcasted_iota(jnp.int32, (rows, columns), 0)
    for s in range(slices):
        lines = add_rows[s].astype(jnp.float32)
        for f in range(frames):
            for o in range(2):
                here = slice(o * columns, (o + 1) * columns)
                value = main[s, f, :, here]
                if f == 0:
                    value = value + add_frames[s, 0, o].astype(jnp.float32)
                if f == frames - 1:
                    value = value + add_frames[s, 1, o].astype(jnp.float32)
                upper = lines[o : o + 1, f * columns : (f + 1) * columns]
                lower = lines[2 + o : 3 + o, f * columns : (f + 1) * columns]
                value = value + jnp.where(row == 0, upper, 0.0)
                value = value + jnp.where(row == rows - 1, lower, 0.0)
                start = (s * frames + f) * rows
                image[start : start + rows, here] = value.astype(jnp.bfloat16)
    size = slices * frames * rows
    for start in range(0, size, 512):
        stop = min(start + 512, size)
        out[:, start:stop] = lax.dot_general(
            table[...], image[start:stop, :], NT, preferred_element_type=jnp.float32
        ).astype(jnp.bfloat16)
    out[:, size:] = jnp.zeros((out.shape[0], out.shape[1] - size), jnp.bfloat16)


def image_to_hybrid(main, add_frames, add_rows, table):
    slices, frames, rows, twice = main.shape
    size = slices * frames * rows
    return pl.pallas_call(
        image_kernel,
        out_shape=jax.ShapeDtypeStruct((twice, -(-size // 128) * 128), jnp.bfloat16),
        scratch_shapes=[pltpu.VMEM((size, twice), jnp.bfloat16)],
        compiler_params=pltpu.CompilerParams(vmem_limit_bytes=VMEM),
        name="image_to_hybrid",
    )(main, add_frames, add_rows, table)


def grad_image_kernel(hybrid, table, out, sums):
    slices, _, frames, rows, columns = out.shape
    sums[...] = jnp.zeros_like(sums)
    for s in range(slices):
        size = frames * rows
        low = s * size // 128 * 128
        high = -(-(s + 1) * size // 128) * 128
        value = lax.dot_general(
            hybrid[:, low:high], table[...], TN, preferred_element_type=jnp.float32
        ).astype(jnp.bfloat16)
        for f in range(frames):
            start = s * size + f * rows - low
            for c in range(2):
                piece = value[start : start + rows, c * columns : (c + 1) * columns]
                out[s, c, f] = piece
                sums[c : c + 1, :] += jnp.sum(piece.astype(jnp.float32), axis=0, keepdims=True)


def hybrid_to_grad(hybrid, table, shape):
    return pl.pallas_call(
        grad_image_kernel,
        out_shape=[
            jax.ShapeDtypeStruct(shape, jnp.bfloat16),
            jax.ShapeDtypeStruct((2, shape[4]), jnp.float32),
        ],
        compiler_params=pltpu.CompilerParams(vmem_limit_bytes=VMEM),
        name="hybrid_to_grad",
    )(hybrid, table)


def chunk_transpose(pieces, low_half, even):
    a, c, b, d = pieces
    a, b = (
        jnp.where(low_half, a, pltpu.roll(b, 64, axis=1)),
        jnp.where(low_half, pltpu.roll(a, 64, axis=1), b),
    )
    c, d = (
        jnp.where(low_half, c, pltpu.roll(d, 64, axis=1)),
        jnp.where(low_half, pltpu.roll(c, 64, axis=1), d),
    )
    return (
        jnp.where(even, a, pltpu.roll(c, 32, axis=1)),
        jnp.where(even, pltpu.roll(a, 96, axis=1), c),
        jnp.where(even, b, pltpu.roll(d, 32, axis=1)),
        jnp.where(even, pltpu.roll(b, 96, axis=1), d),
    )


def kspace_kernel(
    frames_here, received, measured, target, sampled, share, scale, table, out, loss,
    spectrum, grads, loss_lanes,
):
    groups, _, lanes = received.shape
    pairs, n_af, _, twice = spectrum.shape
    rows = twice // 2
    n_row = groups // n_af
    frames = n_af * frames_here
    step = pl.program_id(0)
    lane = lax.broadcasted_iota(jnp.int32, (8, 128), 1)
    low_half = lane < 64
    even = lane % 64 < 32

    @pl.when(step == 0)
    def _():
        loss_lanes[...] = jnp.zeros_like(loss_lanes)

        def gather(af, carry):
            for tile in range(lanes // 128):
                for h in range(n_row // 4):
                    source = [
                        received[af * n_row + h * 4 + m, :, tile * 128 : (tile + 1) * 128].astype(
                            jnp.float32
                        )
                        for m in range(4)
                    ]
                    for c in range(2):
                        moved = chunk_transpose(
                            [one[c * 8 : (c + 1) * 8] for one in source], low_half, even
                        )
                        at = c * rows + h * 128
                        for k in range(4):
                            if tile * 4 + k < pairs:
                                spectrum[tile * 4 + k, af, :, at : at + 128] = moved[k]
            return carry

        lax.fori_loop(0, n_af, gather, 0)

    first = step * frames_here
    size = frames * 8
    here = spectrum[pl.ds(first, frames_here)].reshape(size, twice).astype(jnp.bfloat16)
    kspace = jnp.dot(here, table[...], preferred_element_type=jnp.float32)

    def place(t):
        return (t % frames_here) * n_af + t // frames_here

    filled = []
    for t in range(frames):
        mask = sampled[t]
        filled.append(mask * measured[0, t] + (1.0 - mask) * kspace[place(t) * 8 : place(t) * 8 + 8])
    slopes = []
    for t in range(frames):
        mask = sampled[t]
        near = range(max(t - 2, 0), min(t + 3, frames))
        shared = sum(share[t, s] * filled[s] for s in near)
        differ = mask * measured[0, t] + (1.0 - mask) * shared - target[0, t]
        square = differ * differ + 1.0
        inverse = lax.rsqrt(square)
        loss_lanes[...] += (1.0 - mask) * (square * inverse - 1.0)
        slopes.append((1.0 - mask) * differ * inverse * scale[0, 0])
    for s in range(frames):
        near = range(max(s - 2, 0), min(s + 3, frames))
        grad = sum(share[t, s] * slopes[t] for t in near)
        grads[place(s) * 8 : place(s) * 8 + 8, :] = (1.0 - sampled[s]) * grad
    grad = grads[...]
    high = grad.astype(jnp.bfloat16)
    low = (grad - high.astype(jnp.float32)).astype(jnp.bfloat16)
    back = lax.dot_general(high, table[...], NT, preferred_element_type=jnp.float32)
    back += lax.dot_general(low, table[...], NT, preferred_element_type=jnp.float32)
    spectrum[pl.ds(first, frames_here)] = back.reshape(frames_here, n_af, 8, twice)

    @pl.when(step == pl.num_programs(0) - 1)
    def _():
        loss[...] = loss_lanes[...]

        def scatter(af, carry):
            for tile in range(lanes // 128):
                for h in range(n_row // 4):
                    moved = []
                    for c in range(2):
                        at = c * rows + h * 128
                        moved.append(
                            chunk_transpose(
                                [
                                    spectrum[min(tile * 4 + k, pairs - 1), af, :, at : at + 128]
                                    for k in range(4)
                                ],
                                low_half,
                                even,
                            )
                        )
                    for m in range(4):
                        both = jnp.concatenate([moved[0][m], moved[1][m]], axis=0)
                        out[af * n_row + h * 4 + m, :, tile * 128 : (tile + 1) * 128] = both.astype(
                            jnp.bfloat16
                        )
            return carry

        lax.fori_loop(0, n_af, scatter, 0)


def kspace_step(received, measured, target, sampled, share, scale, table, frames_here):
    slices, frames, lines, twice = measured.shape
    n_af = frames // frames_here
    smem = pl.BlockSpec(memory_space=pltpu.SMEM)
    return pl.pallas_call(
        functools.partial(kspace_kernel, frames_here),
        grid=(slices,),
        in_specs=[
            whole(received.shape),
            a_slice(measured.shape),
            a_slice(target.shape),
            whole(sampled.shape),
            smem,
            smem,
            whole(table.shape),
        ],
        out_specs=[whole(received.shape), whole((lines, twice))],
        out_shape=[
            jax.ShapeDtypeStruct(received.shape, jnp.bfloat16),
            jax.ShapeDtypeStruct((lines, twice), jnp.float32),
        ],
        scratch_shapes=[
            pltpu.VMEM((slices * frames_here, n_af, lines, twice), jnp.float32),
            pltpu.VMEM((frames * lines, twice), jnp.float32),
            pltpu.VMEM((lines, twice), jnp.float32),
        ],
        compiler_params=pltpu.CompilerParams(vmem_limit_bytes=VMEM),
        name="kspace",
    )(received, measured, target, sampled, share, scale, table)


def middle_fast(
    main, add_frames, add_rows, measured, target, sampled, share, scale, table_y, table_x, volume
):
    groups = lax.axis_size("af") * lax.axis_size("row")
    slices, frames_here, rows, twice = main.shape
    lines = measured.shape[2]
    order = np.arange(twice).reshape(2, groups, lines).transpose(1, 0, 2).reshape(-1)
    permuted = jnp.asarray(np.ascontiguousarray(table_y[:, order].T), jnp.bfloat16)
    hybrid = image_to_hybrid(main, add_frames, add_rows, permuted)
    lanes = hybrid.shape[1]
    sent = hybrid.reshape(groups, 2 * lines, lanes)
    received = lax.all_to_all(sent, AXES, 0, 0, tiled=True)
    mask = jnp.broadcast_to(sampled[:, :, None], sampled.shape + (measured.shape[3],))
    back, loss = kspace_step(
        received,
        measured,
        target,
        mask,
        share,
        scale.reshape(1, 1),
        jnp.asarray(table_x, jnp.bfloat16),
        frames_here,
    )
    returned = lax.all_to_all(back, AXES, 0, 0, tiled=True).reshape(twice, lanes)
    grad, sums = hybrid_to_grad(returned, permuted, volume.shape)
    return jnp.sum(loss), grad, jnp.sum(sums, axis=1)


def middle_plain(
    main, add_frames, add_rows, measured, target, sampled, share, scale, table_y, table_x, volume
):
    highest = lax.Precision.HIGHEST
    slices, frames_here, rows_here, twice = main.shape
    columns = twice // 2
    frames, lines = measured.shape[1:3]
    rows = measured.shape[3] // 2
    table_y = jnp.asarray(table_y, jnp.bfloat16)
    table_x = jnp.asarray(table_x, jnp.bfloat16)
    image = main.reshape(slices, frames_here, rows_here, 2, columns)
    edge = jnp.transpose(add_frames.astype(jnp.float32), (1, 0, 3, 2, 4))
    image = image.at[:, 0].add(edge[0]).at[:, frames_here - 1].add(edge[1])
    line = add_rows.astype(jnp.float32).reshape(slices, 2, 2, frames_here, columns)
    line = jnp.transpose(line, (1, 0, 3, 2, 4))
    image = image.at[:, :, 0].add(line[0]).at[:, :, rows_here - 1].add(line[1])
    flat = image.reshape(slices, frames_here, rows_here, twice).astype(jnp.bfloat16)
    hybrid = jnp.dot(flat, table_y, preferred_element_type=jnp.float32).astype(jnp.bfloat16)
    hybrid = hybrid.reshape(slices, frames_here, rows_here, 2, columns)
    part = lax.all_to_all(hybrid, "af", split_axis=4, concat_axis=1, tiled=True)
    spread = lax.all_to_all(part, "row", split_axis=4, concat_axis=2, tiled=True)
    spectrum = jnp.transpose(spread, (0, 1, 4, 3, 2)).reshape(slices, frames, lines, 2 * rows)
    kspace = jnp.dot(spectrum, table_x, preferred_element_type=jnp.float32)
    mask = sampled[None, :, :, None]
    filled = mask * measured + (1.0 - mask) * kspace
    shared = jnp.einsum("ts,bslk->btlk", share, filled, precision=highest)
    differ = mask * measured + (1.0 - mask) * shared - target
    root = jnp.sqrt(differ * differ + 1.0)
    loss = jnp.sum((1.0 - mask) * (root - 1.0))
    slope = (1.0 - mask) * differ / root * scale
    grad = (1.0 - mask) * jnp.einsum("ts,btlk->bslk", share, slope, precision=highest)
    back = jnp.dot(grad, table_x.T.astype(jnp.float32), precision=highest).astype(jnp.bfloat16)
    back = jnp.transpose(back.reshape(slices, frames, lines, 2, rows), (0, 1, 4, 3, 2))
    part = lax.all_to_all(back, "row", split_axis=2, concat_axis=4, tiled=True)
    whole_rows = lax.all_to_all(part, "af", split_axis=1, concat_axis=4, tiled=True)
    grad = jnp.dot(
        whole_rows.reshape(slices, frames_here, rows_here, twice),
        table_y.T,
        preferred_element_type=jnp.float32,
    ).reshape(slices, frames_here, rows_here, 2, columns)
    grad = jnp.transpose(grad, (0, 3, 1, 2, 4)).astype(jnp.bfloat16)
    return loss, grad, jnp.sum(grad.astype(jnp.float32), axis=(0, 2, 3, 4))


def on_device(
    image_in, measured, target, line_mask, window_half, in_kernel, out_kernel, biases,
    in_moment, out_moment, bias_moment, in_square, out_square, bias_square,
    in_smooth, out_smooth, bias_smooth,
):
    slices, _, frames_here, rows_here, columns = image_in.shape
    frames, lines = measured.shape[1:3]
    width = in_kernel.shape[0]
    rows = rows_here * lax.axis_size("row")
    table_y = dft_table(columns)
    table_x = dft_table(rows)
    share = share_matrix(window_half, frames)
    sampled = line_mask.astype(jnp.float32)
    count = lax.psum(jnp.sum(1.0 - sampled) * (2.0 * slices * rows), AXES)
    w_in = conv_in_weights(in_kernel, biases[:width])
    w_out = conv_out_weights(out_kernel)
    w_back = conv_back_weights(out_kernel)

    edge_frames, edge_rows = edges_of(image_in)
    main, part_frames, part_rows = conv_forward(
        image_in, edge_frames, edge_rows, w_in, w_out, biases[width:]
    )
    add_frames, add_rows = return_edges(part_frames, part_rows, columns)
    fits = rows_here == 32 and lines == 8 and lax.axis_size("row") % 4 == 0
    middle = middle_fast if fits else middle_plain
    loss_part, grad_branch, sums = middle(
        main, add_frames, add_rows, measured, target, sampled, share, 1.0 / count,
        table_y, table_x, image_in,
    )
    grad_frames, grad_rows = edges_of(grad_branch)
    sum_in, sum_out = conv_backward(
        image_in, edge_frames, edge_rows, grad_branch, grad_frames, grad_rows, w_in, w_back
    )
    grad_in, bias_in = fold_in(sum_in, width)
    grad_out = fold_out(sum_out, width)
    grad_bias = jnp.concatenate([bias_in, sums])
    grad_in, grad_out, grad_bias, loss_total = lax.psum(
        (grad_in, grad_out, grad_bias, loss_part), AXES
    )
    in_first, in_second, in_master = adam_step(in_kernel, grad_in, in_moment, in_square, rate_in)
    out_first, out_second, out_master = adam_step(
        out_kernel, grad_out, out_moment, out_square, rate_out
    )
    bias_first, bias_second, bias_master = adam_step(
        biases, grad_bias, bias_moment, bias_square, rate_bias
    )
    in_average = average_keep * in_smooth + (1.0 - average_keep) * in_master
    out_average = average_keep * out_smooth + (1.0 - average_keep) * out_master
    bias_average = average_keep * bias_smooth + (1.0 - average_keep) * bias_master
    return (
        loss_total, count,
        in_first, out_first, bias_first,
        in_second, out_second, bias_second,
        in_master, out_master, bias_master,
        in_average, out_average, bias_average,
        in_master.astype(jnp.bfloat16), out_master.astype(jnp.bfloat16), bias_master.astype(jnp.bfloat16),
    )


def solution(mesh):
    in_specs = (
        P(None, None, "af", "row", None),
        P(None, None, ("af", "row"), None),
        P(None, None, ("af", "row"), None),
        P(None, ("af", "row")),
    ) + (P(),) * 13
    return jax.shard_map(
        on_device, mesh=mesh, in_specs=in_specs, out_specs=(P(),) * 17, check_vma=False
    )
```

time: 2630 us -> 468 us (0.18)
  matrix products: 674 us -> 0 us
  local copies, waits for them, and re-layouts: 674 us -> 22.3 us
  blocking collectives: 486 us -> 102 us
  starting transfers between devices: 350 us -> 43.4 us
  waiting for transfers between devices: 323 us -> 60 us
  Pallas kernels: 0 us -> 223 us
  other arithmetic: 69.1 us -> 13 us
  loops' own time: 42.7 us -> 0 us
    dot_general x110 -> x0, matrix products: 674 us -> none  [the longest x10 191 us: micro_step(): jnp.einsum('bkfxy,bcfxy->kc', grad_wide, hidden_pad, preferred_element_ty...]
    all_to_all x30 -> x0, blocking collectives: 402 us -> none  [the longest x10 177 us: micro_step(): lax.all_to_all(hybrid, 'af', split_axis=4, concat_axis=1, tiled=True)]
    ppermute x120 -> x14, starting transfers between devices: 316 us -> 30.5 us  [the longest x2 6.49 us: edges_of(): below = lax.ppermute(volume[:, :, frames - 1], 'af', along('af', 1))]
    ppermute x120 -> x14, waiting for transfers between devices: 266 us -> 19.7 us  [the longest x2 10.6 us: edges_of(): above = lax.ppermute(volume[:, :, 0], 'af', along('af', -1))]
    pallas_call x0 -> x5, Pallas kernels: none -> 223 us  [the longest x1 108 us: conv_backward(): pl.pallas_call(backward_kernel, grid=(slices,), in_specs=[a_slice(one.sha...]
    transpose x10 -> x2, local copies, waits for them, and re-layouts: 223 us -> 0.03 us  [the longest x1 0.02 us: fold_out(): taps[:, ::-1, ::-1, :, ::-1].transpose(1, 4, 2, 3, 0).reshape(27, 2, width)]
    while x1171 -> x0, local copies, waits for them, and re-layouts: 174 us -> none
    slice x50 -> x15, local copies, waits for them, and re-layouts: 163 us -> 7.62 us  [the longest x2 3.2 us: flat(): middle = volume[:, :, :, at].reshape(slices, 2, frames * columns)]
  transfers between devices with their start and end apart: 130 -> 16, of which waited for: 70 -> 9; matrix products, arithmetic and copies ran while one was open for 8% -> 4% of each run, Pallas kernels for 0% -> 0%
where the time goes in v1:
time: 468 us; the launch traced here: 467 us
  Pallas kernels  223 us (48%)
  blocking collectives  102 us (22%)
  waiting for transfers between devices  60 us (13%)
  starting transfers between devices  43.4 us (9%)
  local copies, waits for them, and re-layouts  22.3 us (5%)
  other arithmetic  13 us (3%)
    pallas_call x1, Pallas kernels, conv_backward(): pl.pallas_call(backward_kernel, grid=(slices,), in_specs=[a_slice(one.sha...  108 us
    pallas_call x1, Pallas kernels, conv_forward(): pl.pallas_call(forward_kernel, grid=(slices,), in_specs=[a_slice(own.shap...  76.6 us
    psum x1, blocking collectives, on_device(): count = lax.psum(jnp.sum(1.0 - sampled) * (2.0 * slices * rows), AXES)  59.7 us
    psum x1, blocking collectives, on_device(): lax.psum((grad_in, grad_out, grad_bias, loss_part), AXES)  42.5 us
    all_to_all x1, waiting for transfers between devices, middle_fast(): lax.all_to_all(back, AXES, 0, 0, tiled=True).reshape(twice, lanes)  40.3 us
    pallas_call x1, Pallas kernels, kspace_step(): pl.pallas_call(functools.partial(kspace_kernel, frames_here), grid=(slice...  29.7 us
    ppermute x2, waiting for transfers between devices, edges_of(): above = lax.ppermute(volume[:, :, 0], 'af', along('af', -1))  10.6 us
  transfers between devices with their start and end apart: 16, of which 9 were waited for; matrix products, arithmetic and copies ran while one was open for 4% of the time, Pallas kernels for 0%

profile of v1, /device:TPU:0, one launch (start us, length us, event | category | flops | bytes accessed | tf_op | source)
XLA Modules:
  0.0 466.7 jit_solution(9540407969127415953)
XLA Ops:
  2.2 4.9 %collective-permute-start = (bf16[10,2,32,256]{3,1,0,2:T(2,128)(2,1)S(1)}, bf16[10,2,32,256]{3,1,0,2:T(2,128)(2,1)S(1)}, u32[]{:S(2)}, u32[]{:S(2)}) collective-permute-start(bf16[10,2,32,256]{3,1,0,2:T(2,128)(2,1)S(1)} %bitcast.124), channel_id=1, source_target_pairs={{0,8},{8,16},{16,24},{1,9},{9,17},{17,25},{2,10},{10,18},{18,26},{... | collective-permute-start | bytes 983048 | tf_op jit(solution)/shard_map/ppermute | solution.py:336
  11.9 1.6 slice_reduce_fusion.3
  14.1 4.5 collective-permute-done.1
  23.2 1.7 collective-permute-done.3
  25.7 76.6 %conv_forward.1 = (f32[10,5,32,512]{3,2,1,0:T(8,128)}, bf16[10,2,2,32,256]{4,3,2,1,0:T(8,128)(2,1)}, bf16[10,4,1792]{2,1,0:T(4,128)(2,1)}) custom-call(bf16[10,2,5,32,256]{4,3,2,1,0:T(8,128)(2,1)} %own.3, bf16[10,2,2,32,256]{4,3,2,1,0:T(8,128)(2,1)} %copy.123.edge_frames, bf16[10,4,1792]{2,1,0:T(4,128)(2,1)} %pad_maximum_fusion.6.edge_rows, ...), custom_call_target="tpu_custom_call" | custom-call | tf_op jit(solution)/shard_map/conv_forward/pallas_call | solution.py:284
  104.3 4.5 collective-permute-start.7
  110.0 3.5 collective-permute-start.4
  115.9 4.1 collective-permute-start.8
  121.3 2.1 collective-permute-done.9
  125.7 4.6 image_to_hybrid.1
  130.4 8.5 %all-to-all-start = ((bf16[32,16,1664]{2,1,0:T(8,128)(2,1)}), bf16[32,16,1664]{2,1,0:T(8,128)(2,1)S(1)}, u32[]{:S(2)}, u32[]{:S(2)}) async-start(bf16[32,16,1664]{2,1,0:T(8,128)(2,1)} %bitcast.116), calls=%async_computation | async-start | bytes 3407872 | tf_op jit(solution)/shard_map/all_to_all | solution.py:598
  140.1 59.7 %psum.35 = f32[]{:T(128)} all-reduce(f32[]{:T(128)S(6)} %mul.114), channel_id=1, replica_groups=mesh['af'=4,'row'=8] {'af','row'}, use_global_device_ids=true, to_apply=%region_2.0 | all-reduce | flops 1 | bytes 8 | tf_op jit(solution)/shard_map/psum | solution.py:672
  202.7 29.7 %kspace.1 = (bf16[32,16,1664]{2,1,0:T(8,128)(2,1)}, f32[8,512]{1,0:T(8,128)}) custom-call(bf16[32,16,1664]{2,1,0:T(8,128)(2,1)} %copy-done, f32[10,20,8,512]{3,2,1,0:T(8,128)} %measured.1, f32[10,20,8,512]{3,2,1,0:T(8,128)} %target.1, f32[20,8,512]{2,1,0:T(8,128)} %broadcast_in_dim.2.sampled, f32[20,20]{1,0:T(8,128)} %convert_divide_fusion.share, ...), custom_call_target="tpu_custom_call" | custom-call | tf_op jit(solution)/shard_map/kspace/pallas_call | solution.py:560
  232.4 4.4 all-to-all-start.1
  236.9 40.3 %all-to-all-done.1 = bf16[32,16,1664]{2,1,0:T(8,128)(2,1)S(1)} async-done(((bf16[32,16,1664]{2,1,0:T(8,128)(2,1)}), bf16[32,16,1664]{2,1,0:T(8,128)(2,1)S(1)}, u32[]{:S(2)}, u32[]{:S(2)}) %all-to-all-start.1) | async-done | bytes 1703968 | tf_op jit(solution)/shard_map/all_to_all | solution.py:610
  278.4 4.3 hybrid_to_grad.1
  282.8 3.1 copy.128
  286.4 1.5 collective-permute-start.10
  291.2 1.6 slice_reduce_fusion.1
  293.0 2.8 collective-permute-done.10
  295.8 6.1 %collective-permute-done.11 = bf16[10,2,32,256]{3,1,0,2:T(2,128)(2,1)S(1)} collective-permute-done((bf16[10,2,32,256]{3,1,0,2:T(2,128)(2,1)S(1)}, bf16[10,2,32,256]{3,1,0,2:T(2,128)(2,1)S(1)}, u32[]{:S(2)}, u32[]{:S(2)}) %collective-permute-start.11) | collective-permute-done | bytes 327712 | tf_op jit(solution)/shard_map/ppermute | solution.py:337
  302.0 1.6 collective-permute-start.12
  309.1 107.8 %conv_backward.1 = (f32[256,144]{1,0:T(8,128)}, f32[256,144]{1,0:T(8,128)}) custom-call(bf16[10,2,5,32,256]{4,3,2,1,0:T(8,128)(2,1)} %own.3, bf16[10,2,2,32,256]{4,3,2,1,0:T(8,128)(2,1)} %copy.123.edge_frames, bf16[10,4,1792]{2,1,0:T(4,128)(2,1)} %pad_maximum_fusion.6.edge_rows, bf16[10,2,5,32,256]{4,3,2,1,0:T(8,128)(2,1)} %get-tuple-element.43.grad, ...), custom_call_target="tpu_custom_call" | custom-call | tf_op jit(solution)/shard_map/conv_backward/pallas_call | solution.py:317
  420.5 42.5 %all-reduce.14 = (f32[]{:T(128)}, f32[64,54]{0,1:T(8,128)S(1)}, f32[27,2,64]{2,1,0:T(2,128)S(1)}, f32[66]{0:T(128)S(1)}) all-reduce(f32[]{:T(128)} %reduce_sum.47, f32[64,54]{0,1:T(8,128)S(1)} %reshape.142, f32[27,2,64]{2,1,0:T(2,128)S(1)} %bitcast.137, f32[66]{0:T(128)S(1)} %pad_maximum_fusion.14), channel_id=1, replica_groups=mesh['af'=4,'row'=8] {'af','row'}, use_global_device_ids=true, to_apply=%region_4.5 | all-reduce | flops 6979 | bytes 55832 | tf_op jit(solution)/shard_map/psum | solution.py:695
  (146 shorter events, 41.9 us)
Async XLA Ops:
  2.2 11.9 %collective-permute-start = (bf16[10,2,32,256]{3,1,0,2:T(2,128)(2,1)S(1)}, bf16[10,2,32,256]{3,1,0,2:T(2,128)(2,1)S(1)}, u32[]{:S(2)}, u32[]{:S(2)}) collective-permute-start(bf16[10,2,32,256]{3,1,0,2:T(2,128)(2,1)S(1)} %bitcast.124), channel_id=1, source_target_pairs={{0,8},{8,16},{16,24},{1,9},{9,17},{17,25},{2,10},{10,18},{18,26},{... | collective-permute-start | bytes 983048 | tf_op jit(solution)/shard_map/ppermute | solution.py:336
  7.5 11.1 %collective-permute-start.1 = (bf16[10,2,32,256]{3,1,0,2:T(2,128)(2,1)S(1)}, bf16[10,2,32,256]{3,1,0,2:T(2,128)(2,1)S(1)}, u32[]{:S(2)}, u32[]{:S(2)}) collective-permute-start(bf16[10,2,32,256]{3,1,0,2:T(2,128)(2,1)S(1)} %bitcast.125), channel_id=1, source_target_pairs={{8,0},{16,8},{24,16},{9,1},{17,9},{25,17},{10,2},{18,10},{26,18},{... | collective-permute-start | bytes 983048 | tf_op jit(solution)/shard_map/ppermute | solution.py:337
  18.6 4.6 collective-permute-start.2
  20.0 4.9 %collective-permute-start.3 = (bf16[10,2,1792]{2,1,0:T(2,128)(2,1)S(1)}, bf16[10,2,1792]{2,1,0:T(2,128)(2,1)S(1)}, u32[]{:S(2)}, u32[]{:S(2)}) collective-permute-start(bf16[10,2,1792]{2,1,0:T(2,128)(2,1)S(1)} %pad_maximum_fusion.10), channel_id=1, source_target_pairs={{1,0},{2,1},{3,2},{4,3},{5,4},{6,5},{7,6},{9,8},{10,9},{11,10},{12... | collective-permute-start | bytes 215048 | tf_op jit(solution)/shard_map/ppermute | solution.py:345
  103.0 11.8 %collective-permute-start.6 = (bf16[10,4,256]{2,1,0:T(4,128)(2,1)S(1)}, bf16[10,4,256]{2,1,0:T(4,128)(2,1)S(1)}, u32[]{:S(2)}, u32[]{:S(2)}) collective-permute-start(bf16[10,4,256]{2,1,0:T(4,128)(2,1)S(1)} %get-tuple-element.89), channel_id=1, source_target_pairs={{8,0},{16,8},{24,16},{9,1},{17,9},{25,17},{10,2},{18,10},{26,18},{... | collective-permute-start | bytes 61448 | tf_op jit(solution)/shard_map/ppermute | solution.py:352
  104.3 10.5 %collective-permute-start.7 = (bf16[10,4,256]{2,1,0:T(4,128)(2,1)S(1)}, bf16[10,4,256]{2,1,0:T(4,128)(2,1)S(1)}, u32[]{:S(2)}, u32[]{:S(2)}) collective-permute-start(bf16[10,4,256]{2,1,0:T(4,128)(2,1)S(1)} %get-tuple-element.90), channel_id=1, source_target_pairs={{0,8},{8,16},{16,24},{1,9},{9,17},{17,25},{2,10},{10,18},{18,26},{... | collective-permute-start | bytes 61448 | tf_op jit(solution)/shard_map/ppermute | solution.py:353
  110.0 14.1 %collective-permute-start.4 = (bf16[10,2,32,256]{3,2,1,0:T(8,128)(2,1)S(1)}, bf16[10,2,32,256]{3,2,1,0:T(8,128)(2,1)S(1)}, u32[]{:S(2)}, u32[]{:S(2)}) collective-permute-start(bf16[10,2,32,256]{3,2,1,0:T(8,128)(2,1)S(1)} %get-tuple-element.71), channel_id=1, source_target_pairs={{0,8},{8,16},{16,24},{1,9},{9,17},{17,25},{2,10},{10,18},{18,26},{... | collective-permute-start | bytes 983048 | tf_op jit(solution)/shard_map/ppermute | solution.py:351
  113.5 11.3 %collective-permute-start.5 = (bf16[10,2,32,256]{3,2,1,0:T(8,128)(2,1)S(1)}, bf16[10,2,32,256]{3,2,1,0:T(8,128)(2,1)S(1)}, u32[]{:S(2)}, u32[]{:S(2)}) collective-permute-start(bf16[10,2,32,256]{3,2,1,0:T(8,128)(2,1)S(1)} %get-tuple-element.72), channel_id=1, source_target_pairs={{8,0},{16,8},{24,16},{9,1},{17,9},{25,17},{10,2},{18,10},{26,18},{... | collective-permute-start | bytes 983048 | tf_op jit(solution)/shard_map/ppermute | solution.py:350
  115.9 5.4 %collective-permute-start.8 = (bf16[10,2,1280]{2,1,0:T(2,128)(2,1)S(1)}, bf16[10,2,1280]{2,1,0:T(2,128)(2,1)S(1)}, u32[]{:S(2)}, u32[]{:S(2)}) collective-permute-start(bf16[10,2,1280]{2,1,0:T(2,128)(2,1)S(1)} %get-tuple-element.91), channel_id=1, source_target_pairs={{0,1},{1,2},{2,3},{3,4},{4,5},{5,6},{6,7},{8,9},{9,10},{10,11},{11... | collective-permute-start | bytes 153608 | tf_op jit(solution)/shard_map/ppermute | solution.py:361
  120.0 3.4 collective-permute-start.9
  130.4 70.2 %copy-start.19 = (s32[20]{0:T(128)S(1)}, s32[20]{0:T(128)}, u32[]{:S(2)}) copy-start(s32[20]{0:T(128)} %param.25) | copy-start | bytes 244
  130.4 71.0 %all-to-all-start = ((bf16[32,16,1664]{2,1,0:T(8,128)(2,1)}), bf16[32,16,1664]{2,1,0:T(8,128)(2,1)S(1)}, u32[]{:S(2)}, u32[]{:S(2)}) async-start(bf16[32,16,1664]{2,1,0:T(8,128)(2,1)} %bitcast.116), calls=%async_computation | async-start | bytes 3407872 | tf_op jit(solution)/shard_map/all_to_all | solution.py:598
  232.4 44.8 %all-to-all-start.1 = ((bf16[32,16,1664]{2,1,0:T(8,128)(2,1)}), bf16[32,16,1664]{2,1,0:T(8,128)(2,1)S(1)}, u32[]{:S(2)}, u32[]{:S(2)}) async-start(bf16[32,16,1664]{2,1,0:T(8,128)(2,1)} %get-tuple-element.42), calls=%async_computation.1 | async-start | bytes 3407872 | tf_op jit(solution)/shard_map/all_to_all | solution.py:610
  286.4 9.4 %collective-permute-start.10 = (bf16[10,2,32,256]{3,1,0,2:T(2,128)(2,1)S(1)}, bf16[10,2,32,256]{3,1,0,2:T(2,128)(2,1)S(1)}, u32[]{:S(2)}, u32[]{:S(2)}) collective-permute-start(bf16[10,2,32,256]{3,1,0,2:T(2,128)(2,1)S(1)} %get-tuple-element.67), channel_id=1, source_target_pairs={{0,8},{8,16},{16,24},{1,9},{9,17},{17,25},{2,10},{10,18},{18,26},{... | collective-permute-start | bytes 983048 | tf_op jit(solution)/shard_map/ppermute | solution.py:336
  289.9 12.0 %collective-permute-start.11 = (bf16[10,2,32,256]{3,1,0,2:T(2,128)(2,1)S(1)}, bf16[10,2,32,256]{3,1,0,2:T(2,128)(2,1)S(1)}, u32[]{:S(2)}, u32[]{:S(2)}) collective-permute-start(bf16[10,2,32,256]{3,1,0,2:T(2,128)(2,1)S(1)} %get-tuple-element.68), channel_id=1, source_target_pairs={{8,0},{16,8},{24,16},{9,1},{17,9},{25,17},{10,2},{18,10},{26,18},{... | collective-permute-start | bytes 983048 | tf_op jit(solution)/shard_map/ppermute | solution.py:337
  302.0 4.9 %collective-permute-start.12 = (bf16[10,2,1792]{2,1,0:T(2,128)(2,1)S(1)}, bf16[10,2,1792]{2,1,0:T(2,128)(2,1)S(1)}, u32[]{:S(2)}, u32[]{:S(2)}) collective-permute-start(bf16[10,2,1792]{2,1,0:T(2,128)(2,1)S(1)} %pad_maximum_fusion.11), channel_id=1, source_target_pairs={{0,1},{1,2},{2,3},{3,4},{4,5},{5,6},{6,7},{8,9},{9,10},{10,11},{11... | collective-permute-start | bytes 215048 | tf_op jit(solution)/shard_map/ppermute | solution.py:344
  303.7 4.6 collective-permute-start.13
  418.0 45.6 %copy-start.8 = (f32[64,54]{0,1:T(8,128)S(1)}, f32[64,54]{0,1:T(8,128)}, u32[]{:S(2)}) copy-start(f32[64,54]{0,1:T(8,128)} %param.35) | copy-start | bytes 41476
  418.2 46.1 %copy-start.9 = (f32[27,2,64]{2,1,0:T(2,128)S(1)}, f32[27,2,64]{2,1,0:T(2,128)}, u32[]{:S(2)}) copy-start(f32[27,2,64]{2,1,0:T(2,128)} %param.33) | copy-start | bytes 41476
  418.2 46.1 %copy-start.10 = (f32[27,2,64]{2,1,0:T(2,128)S(1)}, f32[27,2,64]{2,1,0:T(2,128)}, u32[]{:S(2)}) copy-start(f32[27,2,64]{2,1,0:T(2,128)} %param.30) | copy-start | bytes 41476
  418.2 46.7 %copy-start.11 = (f32[27,2,64]{2,1,0:T(2,128)S(1)}, f32[27,2,64]{2,1,0:T(2,128)}, u32[]{:S(2)}) copy-start(f32[27,2,64]{2,1,0:T(2,128)} %param.36) | copy-start | bytes 41476
  418.2 47.4 %copy-start.16 = (f32[66]{0:T(128)S(1)}, f32[66]{0:T(128)}, u32[]{:S(2)}) copy-start(f32[66]{0:T(128)} %param.34) | copy-start | bytes 796
  418.2 47.4 %copy-start.17 = (f32[66]{0:T(128)S(1)}, f32[66]{0:T(128)}, u32[]{:S(2)}) copy-start(f32[66]{0:T(128)} %param.31) | copy-start | bytes 796
  418.3 47.9 %copy-start.20 = (f32[66]{0:T(128)S(1)}, f32[66]{0:T(128)}, u32[]{:S(2)}) copy-start(f32[66]{0:T(128)} %param.37) | copy-start | bytes 796
  (13 other events, 141.3 us)
